TPU v7x, 32 devices: a whole 2x2x4 slice. The times are simulated.
32 devices in a mesh: row: 8 (over z, y), col: 4 (over x, core).
Axes of the slice: x: 2, y: 2, z: 4, core: 2. Of those that a mesh axis runs over, the one named last changes fastest.
Arguments:
- items: bfloat16 [16384, 256], P(('row', 'col')), may hold values from -1.5 to 1.5
- contexts: bfloat16 [8192, 256], P(('col', 'row')), may hold values from -1.5 to 1.5
- tiles: int32 [8, 4, 4, 4], P('row', 'col'), may hold values from 0 to 15, as said below
Outputs:
- item_grads: float32 [16384, 256], P(('row', 'col'))
- context_grads: float32 [8192, 256], P(('col', 'row'))
Inputs may be any that keep to these rules, and one draw needn't show every extreme that they name: tiles[r, c] lists 4 distinct tiles whose item block lies in [r * 2, (r + 1) * 2) and context block in [c * 2, (c + 1) * 2); live slots (both counts 1 to 4) come first, empty slots carry counts 0; each index pair holds 1 to 4 live slots, and the pair 0, 0 holds 4.
All inputs are finite; a program needn't handle non-finite values.
Results may differ from a plain program's by a relative error of at most 0.00042.
Values may be sent and summed in bfloat16 or wider, within the bound.
A program may use at most 64 MiB of HBM per device.

v0:
```python
import jax
import jax.numpy as jnp
from jax import lax
from jax.sharding import PartitionSpec as P

TILE = 1024
RB = 2
CB = 2


def residual_of(scores, entry):
    positive = entry[2].astype(jnp.float32)
    negative = entry[3].astype(jnp.float32)
    factor = 1.0 / TILE**0.5
    return (((positive + negative) * jax.nn.sigmoid(scores) - positive) * factor).astype(
        jnp.bfloat16
    )


def shards(items, contexts, tiles):
    row_pos = lax.axis_index("row")
    col_pos = lax.axis_index("col")
    item_panel = lax.all_gather(items, "col", axis=0, tiled=True)
    context_panel = lax.all_gather(contexts, "row", axis=0, tiled=True)
    entries = tiles.reshape(-1, 4)
    live = jnp.sum(entries[:, 2] + entries[:, 3] > 0)
    row_base = row_pos * RB
    col_base = col_pos * CB

    def blocks(entry):
        item_start = (entry[0] - row_base) * TILE
        context_start = (entry[1] - col_base) * TILE
        return (item_start, context_start)

    def advance(slot, carry):
        grad_items, grad_contexts = carry
        entry = entries[slot]
        item_start, context_start = blocks(entry)
        item_block = lax.dynamic_slice_in_dim(item_panel, item_start, TILE, 0)
        context_block = lax.dynamic_slice_in_dim(context_panel, context_start, TILE, 0)
        scores = jnp.dot(item_block, context_block.T, preferred_element_type=jnp.float32)
        resid = residual_of(scores, entry)
        item_term = jnp.dot(resid, context_block, preferred_element_type=jnp.float32)
        context_term = lax.dot_general(
            resid, item_block, (((0,), (0,)), ((), ())), preferred_element_type=jnp.float32
        )
        old_items = lax.dynamic_slice_in_dim(grad_items, item_start, TILE, 0)
        grad_items = lax.dynamic_update_slice_in_dim(
            grad_items, old_items + item_term, item_start, 0
        )
        old_contexts = lax.dynamic_slice_in_dim(grad_contexts, context_start, TILE, 0)
        grad_contexts = lax.dynamic_update_slice_in_dim(
            grad_contexts, old_contexts + context_term, context_start, 0
        )
        return (grad_items, grad_contexts)

    start = (jnp.zeros(item_panel.shape, jnp.float32), jnp.zeros(context_panel.shape, jnp.float32))
    grad_items, grad_contexts = lax.fori_loop(0, live, advance, start)
    item_grads = lax.psum_scatter(grad_items, "col", scatter_dimension=0, tiled=True)
    context_grads = lax.psum_scatter(grad_contexts, "row", scatter_dimension=0, tiled=True)
    return (item_grads, context_grads)


def solution(mesh):
    placed = (P(("row", "col"), None), P(("col", "row"), None), P("row", "col", None, None))
    return jax.shard_map(
        shards,
        mesh=mesh,
        in_specs=placed,
        out_specs=(P(("row", "col"), None), P(("col", "row"), None)),
        check_vma=False,
    )
```

profile of v0, /device:TPU:0, one launch (start us, length us, event | category | flops | bytes accessed | tf_op | source)
XLA Modules:
  0.0 224.7 jit_solution(14157989276100605972)
XLA Ops:
  7.9 0.7 all-gather.5.cloned.1.call-update
  8.7 1.5 convert_reduce_fusion
  10.2 18.8 %all-gather.3.cloned.1.call-done = bf16[2048,256]{1,0:T(8,128)(2,1)} async-done(((bf16[512,256]{1,0:T(8,128)(2,1)}), bf16[2048,256]{1,0:T(8,128)(2,1)}) %all-gather.3.cloned.1.call-update) | async-done | bytes 1048592 | tf_op jit(solution)/shard_map/all_gather | solution.py:23
  29.0 42.3 %all-gather.5.cloned.1.call-done = bf16[2048,256]{1,0:T(8,128)(2,1)} async-done(((bf16[256,256]{1,0:T(8,128)(2,1)}), bf16[2048,256]{1,0:T(8,128)(2,1)}) %all-gather.5.cloned.1.call-update) | async-done | bytes 1048592 | tf_op jit(solution)/shard_map/all_gather | solution.py:24
  71.5 1.5 broadcast.14
  72.9 43.9 %while.12 = (s32[]{:T(128)}, f32[2048,256]{1,0:T(8,128)}, f32[2048,256]{1,0:T(8,128)S(1)}, s32[]{:T(128)}, s32[4,4]{1,0:T(4,128)}, /*index=5*/s32[]{:T(128)}, bf...) while((s32[]{:T(128)}, f32[2048,256]{1,0:T(8,128)}, ...), condition=%wide.region_2.0_spmd, body=%wide.region_1.0_spmd.sunk | while | flops 1618477056 | bytes 33555440 | solution.py:58
  73.6 0.7 constant_dynamic-slice_fusion.2
  77.4 2.4 %multiply_convert_fusion.2 = bf16[1024,1024]{1,0:T(8,128)(2,1)S(1)} fusion(f32[]{:T(128)} %bitcast.16, f32[]{:T(128)S(6)} %add.61, bf16[2048,256]{1,0:T(8,128)(2,1)} %get-tuple-element.175, s32[]{:T(128)S(6)} %select_n.18, bf16[2048,256]{1,0:T(8,128)(2,1)S(1)} %get-tuple-element.173, s32[]{:T(128)S(6)} %select_n.17), kind=kOutput, calls=%fused_computation.clone.1 | convolution fusion | flops 544210944 | bytes 3146252 | tf_op jit(solution)/shard_map/while/body/dot_general | solution.py:41
  79.8 0.9 fusion.29
  80.6 0.7 copy-done.1
  81.6 0.8 fusion.28
  82.4 1.3 copy-done.2
  84.4 0.7 constant_dynamic-slice_fusion.2
  88.2 2.4 %multiply_convert_fusion.2 = bf16[1024,1024]{1,0:T(8,128)(2,1)S(1)} fusion(f32[]{:T(128)} %bitcast.16, f32[]{:T(128)S(6)} %add.61, bf16[2048,256]{1,0:T(8,128)(2,1)} %get-tuple-element.175, s32[]{:T(128)S(6)} %select_n.18, bf16[2048,256]{1,0:T(8,128)(2,1)S(1)} %get-tuple-element.173, s32[]{:T(128)S(6)} %select_n.17), kind=kOutput, calls=%fused_computation.clone.1 | convolution fusion | flops 544210944 | bytes 3146252 | tf_op jit(solution)/shard_map/while/body/dot_general | solution.py:41
  90.6 0.9 fusion.29
  91.4 0.7 copy-done.1
  92.4 0.8 fusion.28
  93.2 1.3 copy-done.2
  95.2 0.7 constant_dynamic-slice_fusion.2
  99.0 2.4 %multiply_convert_fusion.2 = bf16[1024,1024]{1,0:T(8,128)(2,1)S(1)} fusion(f32[]{:T(128)} %bitcast.16, f32[]{:T(128)S(6)} %add.61, bf16[2048,256]{1,0:T(8,128)(2,1)} %get-tuple-element.175, s32[]{:T(128)S(6)} %select_n.18, bf16[2048,256]{1,0:T(8,128)(2,1)S(1)} %get-tuple-element.173, s32[]{:T(128)S(6)} %select_n.17), kind=kOutput, calls=%fused_computation.clone.1 | convolution fusion | flops 544210944 | bytes 3146252 | tf_op jit(solution)/shard_map/while/body/dot_general | solution.py:41
  101.4 0.9 fusion.29
  102.3 0.7 copy-done.1
  103.2 0.8 fusion.28
  104.0 1.3 copy-done.2
  109.8 2.4 %multiply_convert_fusion.2 = bf16[1024,1024]{1,0:T(8,128)(2,1)S(1)} fusion(f32[]{:T(128)} %bitcast.16, f32[]{:T(128)S(6)} %add.61, bf16[2048,256]{1,0:T(8,128)(2,1)} %get-tuple-element.175, s32[]{:T(128)S(6)} %select_n.18, bf16[2048,256]{1,0:T(8,128)(2,1)S(1)} %get-tuple-element.173, s32[]{:T(128)S(6)} %select_n.17), kind=kOutput, calls=%fused_computation.clone.1 | convolution fusion | flops 544210944 | bytes 3146252 | tf_op jit(solution)/shard_map/while/body/dot_general | solution.py:41
  112.2 0.9 fusion.29
  113.1 0.7 copy-done.1
  114.0 0.8 fusion.28
  114.8 1.3 copy-done.2
  116.8 1.3 copy-done
  118.7 65.9 %reduce-scatter.5.cloned.1.call-done = f32[256,256]{1,0:T(8,128)} async-done(((f32[2048,256]{1,0:T(8,128)}), f32[256,256]{1,0:T(8,128)}) %reduce-scatter.5.cloned.1.call-update) | async-done | bytes 262160 | tf_op jit(solution)/shard_map/reduce_scatter | solution.py:60
  184.6 33.5 %reduce-scatter.3.cloned.1.call-done = f32[512,256]{1,0:T(8,128)} async-done(((f32[2048,256]{1,0:T(8,128)}), f32[512,256]{1,0:T(8,128)}) %reduce-scatter.3.cloned.1.call-update) | async-done | bytes 524304 | tf_op jit(solution)/shard_map/reduce_scatter | solution.py:59
  (32 shorter events, 5.9 us)
Async XLA Ops:
  7.2 21.8 %all-gather.3.cloned.1.call-start = ((), (), s32[]{:S(2)}) async-start(), calls=%async_computation.2 | async-start | bytes 1310720 | tf_op jit(solution)/shard_map/all_gather | solution.py:23
  7.9 63.4 %all-gather.5.cloned.1.call-start = ((), (), s32[]{:S(2)}) async-start(), calls=%async_computation.3 | async-start | bytes 1179648 | tf_op jit(solution)/shard_map/all_gather | solution.py:24
  8.6 176.0 %reduce-scatter.5.cloned.1.call-start = ((), (), s32[]{:S(2)}) async-start(), calls=%async_computation.5 | async-start | bytes 2359296 | tf_op jit(solution)/shard_map/reduce_scatter | solution.py:60
  29.0 43.9 %copy-start.3 = (bf16[2048,256]{1,0:T(8,128)(2,1)S(1)}, bf16[2048,256]{1,0:T(8,128)(2,1)}, u32[]{:S(2)}) copy-start(bf16[2048,256]{1,0:T(8,128)(2,1)} %all-gather.3.cloned.1.call-done) | copy-start | bytes 3145732
  79.8 1.6 copy-start.1
  79.8 1.8 copy-start.4
  82.4 1.3 copy-start.2
  90.6 1.6 copy-start.1
  90.6 1.8 copy-start.4
  93.2 1.3 copy-start.2
  101.4 1.6 copy-start.1
  101.4 1.8 copy-start.4
  104.0 1.3 copy-start.2
  112.2 1.6 copy-start.1
  112.2 1.8 copy-start.4
  114.8 1.3 copy-start.2
  116.8 1.3 copy-start
  118.2 100.0 %reduce-scatter.3.cloned.1.call-start = ((), (), s32[]{:S(2)}) async-start(), calls=%async_computation.4 | async-start | bytes 2621440 | tf_op jit(solution)/shard_map/reduce_scatter | solution.py:59
Sparse Core Ops, SparseCore 0:
  9.6 19.4 all-gather.2
  31.1 40.1 all-gather.4
  118.3 66.2 reduce-scatter.4
  187.6 30.5 reduce-scatter.2
where the time goes:
time: 225 us
  waiting for transfers between devices  162 us (72%)
  local copies, waits for them, and re-layouts  17.5 us (8%)
  matrix products  16 us (7%)
  between operations  13.8 us (6%)
  loops' own time  13.3 us (6%)
    reduce_scatter x1, waiting for transfers between devices, shards(): lax.psum_scatter(grad_contexts, 'row', scatter_dimension=0, tiled=True)  65.9 us
    all_gather x1, waiting for transfers between devices, shards(): context_panel = lax.all_gather(contexts, 'row', axis=0, tiled=True)  42.3 us
    reduce_scatter x1, waiting for transfers between devices, shards(): lax.psum_scatter(grad_items, 'col', scatter_dimension=0, tiled=True)  33.5 us
    all_gather x1, waiting for transfers between devices, shards(): item_panel = lax.all_gather(items, 'col', axis=0, tiled=True)  18.8 us
    another operation x1, loops' own time, shards(): grad_items, grad_contexts = lax.fori_loop(0, live, advance, start)  13.3 us
    dot_general x4, matrix products, advance(): jnp.dot(item_block, context_block.T, preferred_element_type=jnp.float32)  9.43 us
    while x24, local copies, waits for them, and re-layouts  9.2 us
  transfers between devices with their start and end apart: 4, of which 4 were waited for; matrix products, arithmetic and copies ran while one was open for 1% of the time, Pallas kernels for 0%

commit v1 on v0

v1 whole, which is shorter than its diff:
```python
import functools

import jax
import jax.numpy as jnp
from jax import lax
from jax.experimental import pallas as pl
from jax.experimental.pallas import tpu as pltpu
from jax.sharding import PartitionSpec as P

TILE = 1024
RB = 2
CB = 2
SLOTS = 4


def kernel(
    nr, nc, items_ref, ctx_ref, tiles_ref, gi_out, gc_out,
    items_all, ctx_all, gi, gco, gcs, ry, rz, rk, rx, coef,
    s_ic, r_ic, s_ix, r_ix, s_ir, r_ir, s_cy, r_cy, s_cz, r_cz, s_cr, r_cr,
    s_gy, r_gy, s_gz, r_gz, s_ik, r_ik, s_xx, r_xx,
):
    nz, nx = nr // 2, nc // 2
    bi, bc = items_ref.shape[0], ctx_ref.shape[0]
    r = lax.axis_index("row")
    c = lax.axis_index("col")
    z, y = r // 2, r % 2
    x, k = c // 2, c % 2

    def dev(zz, yy, xx, kk):
        return (zz * 2 + yy, xx * 2 + kk)

    def zof(d):
        return lax.rem(z + d, nz)

    def xof(d):
        return lax.rem(x + d, nx)

    ypeer = dev(z, 1 - y, x, k)
    kpeer = dev(z, y, x, 1 - k)

    barrier = pltpu.get_barrier_semaphore()
    peers = [kpeer, ypeer]
    peers += [dev(z, y, xof(e), k) for e in range(1, nx)]
    peers += [dev(zof(e), y, x, k) for e in range(1, nz)]
    for p in peers:
        pl.semaphore_signal(barrier, inc=1, device_id=p, device_id_type=pl.DeviceIdType.MESH)
    pl.semaphore_wait(barrier, len(peers))

    def rcopy(src, dst, ss, rs, to):
        return pltpu.make_async_remote_copy(
            src_ref=src, dst_ref=dst, send_sem=ss, recv_sem=rs,
            device_id=to, device_id_type=pl.DeviceIdType.MESH,
        )

    def islot(i):
        return items_all.at[pl.ds(pl.multiple_of(i * bi, bi), bi)]

    def cslot(j):
        return ctx_all.at[pl.ds(pl.multiple_of(j * bc, bc), bc)]

    c_ic = rcopy(items_ref, islot(c), s_ic, r_ic, kpeer)
    c_cy = rcopy(ctx_ref, cslot(r), s_cy, r_cy, ypeer)

    def c_ix(e):
        return rcopy(items_ref, islot(c), s_ix.at[e], r_ix.at[nx - e], dev(z, y, xof(e), k))

    def c_cz(e):
        return rcopy(ctx_ref, cslot(r), s_cz.at[e], r_cz.at[nz - e], dev(zof(e), y, x, k))

    def c_ir(d):
        blk = islot(xof(d) * 2 + k)
        return rcopy(blk, blk, s_ir.at[d], r_ir.at[d], kpeer)

    def c_cr(d):
        blk = cslot(zof(d) * 2 + y)
        return rcopy(blk, blk, s_cr.at[d], r_cr.at[d], ypeer)

    c_ic.start()
    for e in range(1, nx):
        c_ix(e).start()
    for e in range(1, nz):
        c_cz(e).start()
    c_cy.start()

    items_all[pl.ds(pl.multiple_of(c * bi, bi), bi), :] = items_ref[...]
    ctx_all[pl.ds(pl.multiple_of(r * bc, bc), bc), :] = ctx_ref[...]

    for a in range(RB):
        for b in range(CB):
            pos = jnp.int32(0)
            neg = jnp.int32(0)
            for s in range(SLOTS):
                hit = (tiles_ref[0, 0, s, 0] == r * RB + a) & (tiles_ref[0, 0, s, 1] == c * CB + b)
                pos = pos + jnp.where(hit, tiles_ref[0, 0, s, 2], 0)
                neg = neg + jnp.where(hit, tiles_ref[0, 0, s, 3], 0)
            half = 0.5 / TILE**0.5
            coef[2 * (a * CB + b)] = (pos + neg).astype(jnp.float32) * half
            coef[2 * (a * CB + b) + 1] = (neg - pos).astype(jnp.float32) * half

    def unit(i, j, dst, first_c, first_i):
        cb = ctx_all[pl.ds(pl.multiple_of(j * bc, bc), bc), :]
        rows = pl.ds(pl.multiple_of(i * bi, bi), bi)
        ib = items_all[rows, :]
        at = 2 * ((i // (nc // RB)) * CB + j // (nr // CB))
        amp = coef[at]
        off = coef[at + 1]
        sc = lax.dot_general(ib, cb, (((1,), (1,)), ((), ())), preferred_element_type=jnp.float32)
        res = (jnp.tanh(sc * 0.5) * amp + off).astype(jnp.bfloat16)
        it = jnp.dot(res, cb, preferred_element_type=jnp.float32)
        ct = lax.dot_general(res, ib, (((0,), (0,)), ((), ())), preferred_element_type=jnp.float32)
        if first_i:
            gi[rows, :] = it
        else:
            gi[rows, :] += it
        if first_c:
            dst[...] = ct
        else:
            dst[...] += ct

    def block(j, dst, first_i=False):
        unit(c, j, dst, True, first_i)
        unit(x * 2 + 1 - k, j, dst, False, first_i)

        def step(e, carry):
            unit(xof(e) * 2 + k, j, dst, False, first_i)
            unit(xof(e) * 2 + 1 - k, j, dst, False, first_i)
            return carry

        lax.fori_loop(1, nx, step, 0, unroll=nx <= 2)

    def c_gy(d):
        return rcopy(gcs.at[d], ry.at[d], s_gy.at[d], r_gy.at[d], ypeer)

    def c_gz(d):
        return rcopy(gco.at[d], rz.at[nz - d], s_gz.at[d], r_gz.at[nz - d], dev(zof(d), y, x, k))

    def flush(d):
        c_gy(d).wait_recv()
        gco[d] += ry[d]
        c_gz(d).start()

    first = gco.at[0]
    unit(c, r, first, True, True)
    c_ic.wait_recv()
    unit(x * 2 + 1 - k, r, first, False, True)
    for e in range(1, nx):
        c_ix(nx - e).wait_recv()
        c_ir(e).start()
        unit(xof(e) * 2 + k, r, first, False, True)
    c_cz(nz - 1).wait_recv()
    c_cr(1).start()
    for e in range(1, nx):
        c_ir(e).wait_recv()
        unit(xof(e) * 2 + 1 - k, r, first, False, True)
    c_cy.wait_recv()
    block(z * 2 + 1 - y, gcs.at[0])
    c_gy(0).start()

    def zstep(d, carry):
        block(zof(d) * 2 + y, gco.at[d])

        @pl.when(d + 1 < nz)
        def _():
            c_cz(nz - 1 - d).wait_recv()
            c_cr(d + 1).start()

        c_cr(d).wait_recv()
        block(zof(d) * 2 + 1 - y, gcs.at[d])
        c_gy(d).start()

        @pl.when(d > 1)
        def _():
            flush(d - 1)

        return carry

    lax.fori_loop(1, nz, zstep, 0)

    def c_ik(e):
        rows = pl.ds(pl.multiple_of((xof(e) * 2 + 1 - k) * bi, bi), bi)
        return rcopy(gi.at[rows], rk.at[e], s_ik.at[e], r_ik.at[e], kpeer)

    def c_xx(e):
        rows = pl.ds(pl.multiple_of((xof(e) * 2 + k) * bi, bi), bi)
        return rcopy(gi.at[rows], rx.at[nx - e], s_xx.at[e], r_xx.at[nx - e], dev(z, y, xof(e), k))

    order = list(range(1, nx)) + [0]
    for e in order:
        c_ik(e).start()
    for e in range(1, nx):
        c_ik(e).wait_recv()
        rows = pl.ds(pl.multiple_of((xof(e) * 2 + k) * bi, bi), bi)
        gi[rows, :] += rk[e]
        c_xx(e).start()
    flush(nz - 1)

    c_ik(0).wait_recv()
    acc_i = gi[pl.ds(pl.multiple_of(c * bi, bi), bi), :] + rk[0]
    gi_out[...] = acc_i
    c_gy(0).wait_recv()
    gc_out[...] = gco[0] + ry[0]
    for e in range(1, nz):
        c_gz(nz - e).wait_recv()
        gc_out[...] += rz[e]
    for e in range(1, nx):
        c_xx(nx - e).wait_recv()
        gi_out[...] += rx[e]

    c_ic.wait_send()
    c_cy.wait_send()
    c_gy(0).wait_send()
    c_ik(0).wait_send()
    for e in range(1, nx):
        c_ix(e).wait_send()
        c_ir(e).wait_send()
        c_ik(e).wait_send()
        c_xx(e).wait_send()
    for e in range(1, nz):
        c_cz(e).wait_send()
        c_cr(e).wait_send()
        c_gy(e).wait_send()
        c_gz(e).wait_send()


def shards(nr, nc, items, contexts, tiles):
    bi, dim = items.shape
    bc = contexts.shape[0]
    nz, nx = nr // 2, nc // 2
    f32 = jnp.float32
    dma = pltpu.SemaphoreType.DMA
    pairs = [(), (nx,), (nx,), (), (nz,), (nz,), (nz,), (nz,), (nx,), (nx,)]
    sems = []
    for shape in pairs:
        sems += [dma(shape) if shape else dma] * 2
    vm = pl.BlockSpec(memory_space=pltpu.VMEM)
    return pl.pallas_call(
        functools.partial(kernel, nr, nc),
        out_shape=(
            jax.ShapeDtypeStruct((bi, dim), f32),
            jax.ShapeDtypeStruct((bc, dim), f32),
        ),
        in_specs=[vm, vm, pl.BlockSpec(memory_space=pltpu.SMEM)],
        out_specs=(vm, vm),
        scratch_shapes=[
            pltpu.VMEM((bi * nc, dim), items.dtype),
            pltpu.VMEM((bc * nr, dim), contexts.dtype),
            pltpu.VMEM((bi * nc, dim), f32),
            pltpu.VMEM((nz, bc, dim), f32),
            pltpu.VMEM((nz, bc, dim), f32),
            pltpu.VMEM((nz, bc, dim), f32),
            pltpu.VMEM((nz, bc, dim), f32),
            pltpu.VMEM((nx, bi, dim), f32),
            pltpu.VMEM((nx, bi, dim), f32),
            pltpu.SMEM((2 * RB * CB,), f32),
        ] + sems,
        compiler_params=pltpu.CompilerParams(
            collective_id=0, has_side_effects=True, vmem_limit_bytes=40 * 2**20
        ),
    )(items, contexts, tiles)


def solution(mesh):
    nr, nc = mesh.shape["row"], mesh.shape["col"]
    placed = (P(("row", "col"), None), P(("col", "row"), None), P("row", "col", None, None))
    return jax.shard_map(
        functools.partial(shards, nr, nc),
        mesh=mesh,
        in_specs=placed,
        out_specs=(P(("row", "col"), None), P(("col", "row"), None)),
        check_vma=False,
    )
```

time: 225 us -> 65.4 us (0.29)
  waiting for transfers between devices: 162 us -> 0 us
  Pallas kernels: 0 us -> 60.6 us
  matrix products: 16 us -> 0 us
  local copies, waits for them, and re-layouts: 17.5 us -> 4.03 us
  loops' own time: 13.3 us -> 0 us
  between operations: 13.8 us -> 0.65 us
    reduce_scatter x2 -> x0, waiting for transfers between devices: 99.4 us -> none  [the longest x1 65.9 us: shards(): lax.psum_scatter(grad_contexts, 'row', scatter_dimension=0, tiled=True)]
    all_gather x2 -> x0, waiting for transfers between devices: 61.2 us -> none  [the longest x1 42.3 us: shards(): context_panel = lax.all_gather(contexts, 'row', axis=0, tiled=True)]
    pallas_call x0 -> x1, Pallas kernels: none -> 60.6 us  [shards(): pl.pallas_call(functools.partial(kernel, nr, nc), out_shape=(jax.ShapeDty...]
    dot_general x12 -> x0, matrix products: 16 us -> none  [the longest x4 9.43 us: advance(): jnp.dot(item_block, context_block.T, preferred_element_type=jnp.float32)]
    another operation x1 -> x0, loops' own time: 13.3 us -> none  [shards(): grad_items, grad_contexts = lax.fori_loop(0, live, advance, start)]
    while x24 -> x0, local copies, waits for them, and re-layouts: 9.2 us -> none
    dynamic_slice x4 -> x0, local copies, waits for them, and re-layouts: 2.76 us -> none  [advance(): entry = entries[slot]]
    unnamed x4 -> x8, local copies, waits for them, and re-layouts: 1.32 us -> 4.03 us
  transfers between devices with their start and end apart: 4 -> 0, of which waited for: 4 -> 0; matrix products, arithmetic and copies ran while one was open for 1% -> 0% of each run, Pallas kernels for 0% -> 0%
where the time goes in v1:
time: 65.4 us; the launch traced here: 65.2 us
  Pallas kernels  60.6 us (93%)
  local copies, waits for them, and re-layouts  4.03 us (6%)
    pallas_call x1, Pallas kernels, shards(): pl.pallas_call(functools.partial(kernel, nr, nc), out_shape=(jax.ShapeDty...  60.6 us
    unnamed x8, local copies, waits for them, and re-layouts  4.03 us

profile of v1, /device:TPU:0, one launch (start us, length us, event | category | flops | bytes accessed | tf_op | source)
XLA Modules:
  0.0 65.2 jit_solution(6167030654522078728)
XLA Ops:
  0.6 0.0 copy-start
  0.6 0.9 %copy-done = bf16[512,256]{1,0:T(8,128)(2,1)S(1)} copy-done((bf16[512,256]{1,0:T(8,128)(2,1)S(1)}, bf16[512,256]{1,0:T(8,128)(2,1)}, u32[]{:S(2)}) %copy-start) | copy-done | bytes 262168
  1.6 0.0 copy-start.1
  1.6 0.9 %copy-done.1 = bf16[256,256]{1,0:T(8,128)(2,1)S(1)} copy-done((bf16[256,256]{1,0:T(8,128)(2,1)S(1)}, bf16[256,256]{1,0:T(8,128)(2,1)}, u32[]{:S(2)}) %copy-start.1) | copy-done | bytes 131096
  2.5 0.0 copy-start.2
  2.5 0.7 %copy-done.2 = s32[1,1,4,4]{3,2,1,0:T(4,128)S(1)} copy-done((s32[1,1,4,4]{3,2,1,0:T(4,128)S(1)}, s32[1,1,4,4]{3,2,1,0:T(4,128)}, u32[]{:S(2)}) %copy-start.2) | copy-done | bytes 88
  3.2 60.6 %shard_map.50 = (f32[512,256]{1,0:T(8,128)S(1)}, f32[256,256]{1,0:T(8,128)S(1)}) custom-call(bf16[512,256]{1,0:T(8,128)(2,1)S(1)} %copy-done, bf16[256,256]{1,0:T(8,128)(2,1)S(1)} %copy-done.1, s32[1,1,4,4]{3,2,1,0:T(4,128)S(1)} %copy-done.2), custom_call_target="tpu_custom_call" | custom-call | tf_op jit(solution)/shard_map/pallas_call | solution.py:236
  63.7 0.8 %copy.7 = f32[512,256]{1,0:T(8,128)} copy(f32[512,256]{1,0:T(8,128)S(1)} %get-tuple-element.4) | data formatting | bytes 1048576
  64.5 0.7 %copy.8 = f32[256,256]{1,0:T(8,128)} copy(f32[256,256]{1,0:T(8,128)S(1)} %get-tuple-element.5) | data formatting | bytes 524288
Async XLA Ops:
  0.6 1.0 %copy-start = (bf16[512,256]{1,0:T(8,128)(2,1)S(1)}, bf16[512,256]{1,0:T(8,128)(2,1)}, u32[]{:S(2)}) copy-start(bf16[512,256]{1,0:T(8,128)(2,1)} %items_ref.1) | copy-start | bytes 786436
  1.6 0.9 %copy-start.1 = (bf16[256,256]{1,0:T(8,128)(2,1)S(1)}, bf16[256,256]{1,0:T(8,128)(2,1)}, u32[]{:S(2)}) copy-start(bf16[256,256]{1,0:T(8,128)(2,1)} %ctx_ref.1) | copy-start | bytes 393220
  2.5 0.7 %copy-start.2 = (s32[1,1,4,4]{3,2,1,0:T(4,128)S(1)}, s32[1,1,4,4]{3,2,1,0:T(4,128)}, u32[]{:S(2)}) copy-start(s32[1,1,4,4]{3,2,1,0:T(4,128)} %tiles_ref.1) | copy-start | bytes 196

commit v2 on v1

--- a/solution.py
+++ b/solution.py
@@ -11,13 +11,48 @@
 RB = 2
 CB = 2
 SLOTS = 4
+LEVELS = 32766.0
+
+
+class Both:
+    def __init__(self, *copies):
+        self.copies = copies
+
+    def start(self):
+        for one in self.copies:
+            one.start()
+
+    def wait_recv(self):
+        for one in self.copies:
+            one.wait_recv()
+
+    def wait_send(self):
+        for one in self.copies:
+            one.wait_send()
+
+
+def encode(value, codes, peaks):
+    rows, dim = value.shape
+    cube = value.reshape(rows // 8, 8, dim)
+    peak = jnp.maximum(jnp.max(jnp.abs(cube), axis=0), 1e-30)
+    peaks[...] = peak * (1.0 / LEVELS)
+    scaled = jnp.round(cube * (LEVELS / peak)[None]).reshape(rows, dim)
+    codes[...] = scaled.astype(jnp.int32).astype(jnp.int16)
+
+
+def decode(codes, peaks):
+    rows, dim = codes.shape
+    cube = codes.astype(jnp.int32).astype(jnp.float32).reshape(rows // 8, 8, dim)
+    return (cube * peaks[None]).reshape(rows, dim)
 
 
 def kernel(
     nr, nc, items_ref, ctx_ref, tiles_ref, gi_out, gc_out,
-    items_all, ctx_all, gi, gco, gcs, ry, rz, rk, rx, coef,
+    items_all, ctx_all, gi, gco, gct, coef,
+    qy, ry, qz, rz, qk, rk, qx, rx, my, ny, mz, nz_, mk, nk, mx, nx_,
     s_ic, r_ic, s_ix, r_ix, s_ir, r_ir, s_cy, r_cy, s_cz, r_cz, s_cr, r_cr,
     s_gy, r_gy, s_gz, r_gz, s_ik, r_ik, s_xx, r_xx,
+    s_my, r_my, s_mz, r_mz, s_mk, r_mk, s_mx, r_mx,
 ):
     nz, nx = nr // 2, nc // 2
     bi, bc = items_ref.shape[0], ctx_ref.shape[0]
@@ -129,14 +164,21 @@
         lax.fori_loop(1, nx, step, 0, unroll=nx <= 2)
 
     def c_gy(d):
-        return rcopy(gcs.at[d], ry.at[d], s_gy.at[d], r_gy.at[d], ypeer)
+        return Both(
+            rcopy(qy.at[d], ry.at[d], s_gy.at[d], r_gy.at[d], ypeer),
+            rcopy(my.at[d], ny.at[d], s_my.at[d], r_my.at[d], ypeer),
+        )
 
     def c_gz(d):
-        return rcopy(gco.at[d], rz.at[nz - d], s_gz.at[d], r_gz.at[nz - d], dev(zof(d), y, x, k))
+        to, e = dev(zof(d), y, x, k), nz - d
+        return Both(
+            rcopy(qz.at[d], rz.at[e], s_gz.at[d], r_gz.at[e], to),
+            rcopy(mz.at[d], nz_.at[e], s_mz.at[d], r_mz.at[e], to),
+        )
 
     def flush(d):
         c_gy(d).wait_recv()
-        gco[d] += ry[d]
+        encode(gco[d] + decode(ry[d], ny[d]), qz.at[d], mz.at[d])
         c_gz(d).start()
 
     first = gco.at[0]
@@ -153,7 +195,8 @@
         c_ir(e).wait_recv()
         unit(xof(e) * 2 + 1 - k, r, first, False, True)
     c_cy.wait_recv()
-    block(z * 2 + 1 - y, gcs.at[0])
+    block(z * 2 + 1 - y, gct)
+    encode(gct[...], qy.at[0], my.at[0])
     c_gy(0).start()
 
     def zstep(d, carry):
@@ -165,7 +208,8 @@
             c_cr(d + 1).start()
 
         c_cr(d).wait_recv()
-        block(zof(d) * 2 + 1 - y, gcs.at[d])
+        block(zof(d) * 2 + 1 - y, gct)
+        encode(gct[...], qy.at[d], my.at[d])
         c_gy(d).start()
 
         @pl.when(d > 1)
@@ -176,35 +220,41 @@
 
     lax.fori_loop(1, nz, zstep, 0)
 
+    def rows_of(i):
+        return pl.ds(pl.multiple_of(i * bi, bi), bi)
+
     def c_ik(e):
-        rows = pl.ds(pl.multiple_of((xof(e) * 2 + 1 - k) * bi, bi), bi)
-        return rcopy(gi.at[rows], rk.at[e], s_ik.at[e], r_ik.at[e], kpeer)
+        return Both(
+            rcopy(qk.at[e], rk.at[e], s_ik.at[e], r_ik.at[e], kpeer),
+            rcopy(mk.at[e], nk.at[e], s_mk.at[e], r_mk.at[e], kpeer),
+        )
 
     def c_xx(e):
-        rows = pl.ds(pl.multiple_of((xof(e) * 2 + k) * bi, bi), bi)
-        return rcopy(gi.at[rows], rx.at[nx - e], s_xx.at[e], r_xx.at[nx - e], dev(z, y, xof(e), k))
-
-    order = list(range(1, nx)) + [0]
-    for e in order:
+        to, f = dev(z, y, xof(e), k), nx - e
+        return Both(
+            rcopy(qx.at[e], rx.at[f], s_xx.at[e], r_xx.at[f], to),
+            rcopy(mx.at[e], nx_.at[f], s_mx.at[e], r_mx.at[f], to),
+        )
+
+    for e in list(range(1, nx)) + [0]:
+        encode(gi[rows_of(xof(e) * 2 + 1 - k), :], qk.at[e], mk.at[e])
         c_ik(e).start()
     for e in range(1, nx):
         c_ik(e).wait_recv()
-        rows = pl.ds(pl.multiple_of((xof(e) * 2 + k) * bi, bi), bi)
-        gi[rows, :] += rk[e]
+        encode(gi[rows_of(xof(e) * 2 + k), :] + decode(rk[e], nk[e]), qx.at[e], mx.at[e])
         c_xx(e).start()
     flush(nz - 1)
 
     c_ik(0).wait_recv()
-    acc_i = gi[pl.ds(pl.multiple_of(c * bi, bi), bi), :] + rk[0]
-    gi_out[...] = acc_i
+    gi_out[...] = gi[rows_of(c), :] + decode(rk[0], nk[0])
     c_gy(0).wait_recv()
-    gc_out[...] = gco[0] + ry[0]
+    gc_out[...] = gco[0] + decode(ry[0], ny[0])
     for e in range(1, nz):
         c_gz(nz - e).wait_recv()
-        gc_out[...] += rz[e]
+        gc_out[...] += decode(rz[e], nz_[e])
     for e in range(1, nx):
         c_xx(nx - e).wait_recv()
-        gi_out[...] += rx[e]
+        gi_out[...] += decode(rx[e], nx_[e])
 
     c_ic.wait_send()
     c_cy.wait_send()
@@ -229,6 +279,7 @@
     f32 = jnp.float32
     dma = pltpu.SemaphoreType.DMA
     pairs = [(), (nx,), (nx,), (), (nz,), (nz,), (nz,), (nz,), (nx,), (nx,)]
+    pairs += [(nz,), (nz,), (nx,), (nx,)]
     sems = []
     for shape in pairs:
         sems += [dma(shape) if shape else dma] * 2
@@ -246,13 +297,14 @@
             pltpu.VMEM((bc * nr, dim), contexts.dtype),
             pltpu.VMEM((bi * nc, dim), f32),
             pltpu.VMEM((nz, bc, dim), f32),
-            pltpu.VMEM((nz, bc, dim), f32),
-            pltpu.VMEM((nz, bc, dim), f32),
-            pltpu.VMEM((nz, bc, dim), f32),
-            pltpu.VMEM((nx, bi, dim), f32),
-            pltpu.VMEM((nx, bi, dim), f32),
+            pltpu.VMEM((bc, dim), f32),
             pltpu.SMEM((2 * RB * CB,), f32),
-        ] + sems,
+        ]
+        + [pltpu.VMEM((nz, bc, dim), jnp.int16)] * 4
+        + [pltpu.VMEM((nx, bi, dim), jnp.int16)] * 4
+        + [pltpu.VMEM((nz, 8, dim), f32)] * 4
+        + [pltpu.VMEM((nx, 8, dim), f32)] * 4
+        + sems,
         compiler_params=pltpu.CompilerParams(
             collective_id=0, has_side_effects=True, vmem_limit_bytes=40 * 2**20
         ),

time: 65.4 us -> 50.7 us (0.78)
  Pallas kernels: 60.6 us -> 45.8 us
    pallas_call x1, Pallas kernels: 60.6 us -> 45.8 us  [shards(): pl.pallas_call(functools.partial(kernel, nr, nc), out_shape=(jax.ShapeDty...]
where the time goes in v2:
time: 50.7 us; the launch traced here: 50.5 us
  Pallas kernels  45.8 us (90%)
  local copies, waits for them, and re-layouts  4.03 us (8%)
  between operations  0.65 us (1%)
    pallas_call x1, Pallas kernels, shards(): pl.pallas_call(functools.partial(kernel, nr, nc), out_shape=(jax.ShapeDty...  45.8 us
    unnamed x8, local copies, waits for them, and re-layouts  4.03 us

profile of v2, /device:TPU:0, one launch (start us, length us, event | category | flops | bytes accessed | tf_op | source)
XLA Modules:
  0.0 50.5 jit_solution(16122686925010352625)
XLA Ops:
  0.6 0.0 copy-start
  0.6 0.9 %copy-done = bf16[512,256]{1,0:T(8,128)(2,1)S(1)} copy-done((bf16[512,256]{1,0:T(8,128)(2,1)S(1)}, bf16[512,256]{1,0:T(8,128)(2,1)}, u32[]{:S(2)}) %copy-start) | copy-done | bytes 262168
  1.6 0.0 copy-start.1
  1.6 0.9 %copy-done.1 = bf16[256,256]{1,0:T(8,128)(2,1)S(1)} copy-done((bf16[256,256]{1,0:T(8,128)(2,1)S(1)}, bf16[256,256]{1,0:T(8,128)(2,1)}, u32[]{:S(2)}) %copy-start.1) | copy-done | bytes 131096
  2.5 0.0 copy-start.2
  2.5 0.7 %copy-done.2 = s32[1,1,4,4]{3,2,1,0:T(4,128)S(1)} copy-done((s32[1,1,4,4]{3,2,1,0:T(4,128)S(1)}, s32[1,1,4,4]{3,2,1,0:T(4,128)}, u32[]{:S(2)}) %copy-start.2) | copy-done | bytes 88
  3.2 45.8 %shard_map.50 = (f32[512,256]{1,0:T(8,128)S(1)}, f32[256,256]{1,0:T(8,128)S(1)}) custom-call(bf16[512,256]{1,0:T(8,128)(2,1)S(1)} %copy-done, bf16[256,256]{1,0:T(8,128)(2,1)S(1)} %copy-done.1, s32[1,1,4,4]{3,2,1,0:T(4,128)S(1)} %copy-done.2), custom_call_target="tpu_custom_call" | custom-call | tf_op jit(solution)/shard_map/pallas_call | solution.py:287
  49.0 0.8 %copy.7 = f32[512,256]{1,0:T(8,128)} copy(f32[512,256]{1,0:T(8,128)S(1)} %get-tuple-element.4) | data formatting | bytes 1048576
  49.8 0.7 %copy.8 = f32[256,256]{1,0:T(8,128)} copy(f32[256,256]{1,0:T(8,128)S(1)} %get-tuple-element.5) | data formatting | bytes 524288
Async XLA Ops:
  0.6 1.0 %copy-start = (bf16[512,256]{1,0:T(8,128)(2,1)S(1)}, bf16[512,256]{1,0:T(8,128)(2,1)}, u32[]{:S(2)}) copy-start(bf16[512,256]{1,0:T(8,128)(2,1)} %items_ref.1) | copy-start | bytes 786436
  1.6 0.9 %copy-start.1 = (bf16[256,256]{1,0:T(8,128)(2,1)S(1)}, bf16[256,256]{1,0:T(8,128)(2,1)}, u32[]{:S(2)}) copy-start(bf16[256,256]{1,0:T(8,128)(2,1)} %ctx_ref.1) | copy-start | bytes 393220
  2.5 0.7 %copy-start.2 = (s32[1,1,4,4]{3,2,1,0:T(4,128)S(1)}, s32[1,1,4,4]{3,2,1,0:T(4,128)}, u32[]{:S(2)}) copy-start(s32[1,1,4,4]{3,2,1,0:T(4,128)} %tiles_ref.1) | copy-start | bytes 196

commit v3 on v2

--- a/solution.py
+++ b/solution.py
@@ -110,12 +110,11 @@
         blk = cslot(zof(d) * 2 + y)
         return rcopy(blk, blk, s_cr.at[d], r_cr.at[d], ypeer)
 
+    for e in range(1, nx):
+        c_ix(e).start()
+    c_cz(nz - 1).start()
+    c_cy.start()
     c_ic.start()
-    for e in range(1, nx):
-        c_ix(e).start()
-    for e in range(1, nz):
-        c_cz(e).start()
-    c_cy.start()
 
     items_all[pl.ds(pl.multiple_of(c * bi, bi), bi), :] = items_ref[...]
     ctx_all[pl.ds(pl.multiple_of(r * bc, bc), bc), :] = ctx_ref[...]
@@ -185,28 +184,34 @@
     unit(c, r, first, True, True)
     c_ic.wait_recv()
     unit(x * 2 + 1 - k, r, first, False, True)
+    c_cz(nz - 1).wait_send()
+    if nz > 2:
+        c_cz(nz - 2).start()
+    c_cz(nz - 1).wait_recv()
+    c_cr(1).start()
     for e in range(1, nx):
         c_ix(nx - e).wait_recv()
         c_ir(e).start()
         unit(xof(e) * 2 + k, r, first, False, True)
-    c_cz(nz - 1).wait_recv()
-    c_cr(1).start()
     for e in range(1, nx):
         c_ir(e).wait_recv()
         unit(xof(e) * 2 + 1 - k, r, first, False, True)
     c_cy.wait_recv()
     block(z * 2 + 1 - y, gct)
     encode(gct[...], qy.at[0], my.at[0])
-    c_gy(0).start()
 
     def zstep(d, carry):
-        block(zof(d) * 2 + y, gco.at[d])
+        @pl.when(d + 2 < nz)
+        def _():
+            c_cz(nz - 1 - d).wait_send()
+            c_cz(nz - 2 - d).start()
 
         @pl.when(d + 1 < nz)
         def _():
             c_cz(nz - 1 - d).wait_recv()
             c_cr(d + 1).start()
 
+        block(zof(d) * 2 + y, gco.at[d])
         c_cr(d).wait_recv()
         block(zof(d) * 2 + 1 - y, gct)
         encode(gct[...], qy.at[d], my.at[d])
@@ -219,6 +224,7 @@
         return carry
 
     lax.fori_loop(1, nz, zstep, 0)
+    c_gy(0).start()
 
     def rows_of(i):
         return pl.ds(pl.multiple_of(i * bi, bi), bi)
@@ -265,8 +271,8 @@
         c_ir(e).wait_send()
         c_ik(e).wait_send()
         c_xx(e).wait_send()
+    c_cz(1).wait_send()
     for e in range(1, nz):
-        c_cz(e).wait_send()
         c_cr(e).wait_send()
         c_gy(e).wait_send()
         c_gz(e).wait_send()

time: 50.7 us -> 45.4 us (0.90)
  Pallas kernels: 45.8 us -> 40.5 us
    pallas_call x1, Pallas kernels: 45.8 us -> 40.5 us  [shards(): pl.pallas_call(functools.partial(kernel, nr, nc), out_shape=(jax.ShapeDty...]
where the time goes in v3:
time: 45.4 us; the launch traced here: 45.2 us
  Pallas kernels  40.5 us (89%)
  local copies, waits for them, and re-layouts  4.03 us (9%)
  between operations  0.65 us (1%)
    pallas_call x1, Pallas kernels, shards(): pl.pallas_call(functools.partial(kernel, nr, nc), out_shape=(jax.ShapeDty...  40.5 us
    unnamed x8, local copies, waits for them, and re-layouts  4.03 us

profile of v3, /device:TPU:0, one launch (start us, length us, event | category | flops | bytes accessed | tf_op | source)
XLA Modules:
  0.0 45.2 jit_solution(11571136122235558326)
XLA Ops:
  0.6 0.0 copy-start
  0.6 0.9 %copy-done = bf16[512,256]{1,0:T(8,128)(2,1)S(1)} copy-done((bf16[512,256]{1,0:T(8,128)(2,1)S(1)}, bf16[512,256]{1,0:T(8,128)(2,1)}, u32[]{:S(2)}) %copy-start) | copy-done | bytes 262168
  1.6 0.0 copy-start.1
  1.6 0.9 %copy-done.1 = bf16[256,256]{1,0:T(8,128)(2,1)S(1)} copy-done((bf16[256,256]{1,0:T(8,128)(2,1)S(1)}, bf16[256,256]{1,0:T(8,128)(2,1)}, u32[]{:S(2)}) %copy-start.1) | copy-done | bytes 131096
  2.5 0.0 copy-start.2
  2.5 0.7 %copy-done.2 = s32[1,1,4,4]{3,2,1,0:T(4,128)S(1)} copy-done((s32[1,1,4,4]{3,2,1,0:T(4,128)S(1)}, s32[1,1,4,4]{3,2,1,0:T(4,128)}, u32[]{:S(2)}) %copy-start.2) | copy-done | bytes 88
  3.2 40.5 %shard_map.50 = (f32[512,256]{1,0:T(8,128)S(1)}, f32[256,256]{1,0:T(8,128)S(1)}) custom-call(bf16[512,256]{1,0:T(8,128)(2,1)S(1)} %copy-done, bf16[256,256]{1,0:T(8,128)(2,1)S(1)} %copy-done.1, s32[1,1,4,4]{3,2,1,0:T(4,128)S(1)} %copy-done.2), custom_call_target="tpu_custom_call" | custom-call | tf_op jit(solution)/shard_map/pallas_call | solution.py:293
  43.7 0.8 %copy.7 = f32[512,256]{1,0:T(8,128)} copy(f32[512,256]{1,0:T(8,128)S(1)} %get-tuple-element.4) | data formatting | bytes 1048576
  44.5 0.7 %copy.8 = f32[256,256]{1,0:T(8,128)} copy(f32[256,256]{1,0:T(8,128)S(1)} %get-tuple-element.5) | data formatting | bytes 524288
Async XLA Ops:
  0.6 1.0 %copy-start = (bf16[512,256]{1,0:T(8,128)(2,1)S(1)}, bf16[512,256]{1,0:T(8,128)(2,1)}, u32[]{:S(2)}) copy-start(bf16[512,256]{1,0:T(8,128)(2,1)} %items_ref.1) | copy-start | bytes 786436
  1.6 0.9 %copy-start.1 = (bf16[256,256]{1,0:T(8,128)(2,1)S(1)}, bf16[256,256]{1,0:T(8,128)(2,1)}, u32[]{:S(2)}) copy-start(bf16[256,256]{1,0:T(8,128)(2,1)} %ctx_ref.1) | copy-start | bytes 393220
  2.5 0.7 %copy-start.2 = (s32[1,1,4,4]{3,2,1,0:T(4,128)S(1)}, s32[1,1,4,4]{3,2,1,0:T(4,128)}, u32[]{:S(2)}) copy-start(s32[1,1,4,4]{3,2,1,0:T(4,128)} %tiles_ref.1) | copy-start | bytes 196

commit v4 on v3

--- a/solution.py
+++ b/solution.py
@@ -99,8 +99,43 @@
     def c_ix(e):
         return rcopy(items_ref, islot(c), s_ix.at[e], r_ix.at[nx - e], dev(z, y, xof(e), k))
 
-    def c_cz(e):
-        return rcopy(ctx_ref, cslot(r), s_cz.at[e], r_cz.at[nz - e], dev(zof(e), y, x, k))
+    def dord(t):
+        low, high = z, nz - 1 - z
+        both = jnp.minimum(low, high)
+        pair = ((t + 1) // 2) * (1 - 2 * ((t + 1) % 2))
+        far = (t - both) * jnp.where(high > low, 1, -1)
+        return lax.rem(jnp.where(t <= 2 * both, pair, far) + nz, nz)
+
+    def c_line(zz, sign, sem, src=None):
+        blk = cslot(zz * 2 + y)
+        return rcopy(src if src is not None else blk, blk, s_cz.at[sem], r_cz.at[zz], dev(z + sign, y, x, k))
+
+    def own_line(act):
+        @pl.when(z < nz - 1)
+        def _():
+            act(c_line(z, 1, z, ctx_ref))
+
+        @pl.when(z > 0)
+        def _():
+            act(c_line(z, -1, nz, ctx_ref))
+
+    def pass_line(t, act):
+        zz = zof(dord(t))
+
+        @pl.when((zz < z) & (z < nz - 1))
+        def _():
+            act(c_line(zz, 1, zz))
+
+        @pl.when((zz > z) & (z > 0))
+        def _():
+            act(c_line(zz, -1, zz))
+
+    def arrive(t):
+        d = dord(t)
+        blk = cslot(zof(d) * 2 + y)
+        rcopy(blk, blk, s_cz.at[zof(d)], r_cz.at[zof(d)], ypeer).wait_recv()
+        pass_line(t, lambda copy: copy.start())
+        c_cr(d).start()
 
     def c_ir(d):
         blk = islot(xof(d) * 2 + k)
@@ -112,7 +147,7 @@
 
     for e in range(1, nx):
         c_ix(e).start()
-    c_cz(nz - 1).start()
+    own_line(lambda copy: copy.start())
     c_cy.start()
     c_ic.start()
 
@@ -184,11 +219,8 @@
     unit(c, r, first, True, True)
     c_ic.wait_recv()
     unit(x * 2 + 1 - k, r, first, False, True)
-    c_cz(nz - 1).wait_send()
-    if nz > 2:
-        c_cz(nz - 2).start()
-    c_cz(nz - 1).wait_recv()
-    c_cr(1).start()
+    for t in range(1, min(nz, 3)):
+        arrive(t)
     for e in range(1, nx):
         c_ix(nx - e).wait_recv()
         c_ir(e).start()
@@ -200,16 +232,12 @@
     block(z * 2 + 1 - y, gct)
     encode(gct[...], qy.at[0], my.at[0])
 
-    def zstep(d, carry):
-        @pl.when(d + 2 < nz)
-        def _():
-            c_cz(nz - 1 - d).wait_send()
-            c_cz(nz - 2 - d).start()
-
-        @pl.when(d + 1 < nz)
-        def _():
-            c_cz(nz - 1 - d).wait_recv()
-            c_cr(d + 1).start()
+    def zstep(t, carry):
+        d = dord(t)
+
+        @pl.when(t + 2 < nz)
+        def _():
+            arrive(t + 2)
 
         block(zof(d) * 2 + y, gco.at[d])
         c_cr(d).wait_recv()
@@ -217,9 +245,9 @@
         encode(gct[...], qy.at[d], my.at[d])
         c_gy(d).start()
 
-        @pl.when(d > 1)
-        def _():
-            flush(d - 1)
+        @pl.when(t > 1)
+        def _():
+            flush(dord(t - 1))
 
         return carry
 
@@ -249,7 +277,7 @@
         c_ik(e).wait_recv()
         encode(gi[rows_of(xof(e) * 2 + k), :] + decode(rk[e], nk[e]), qx.at[e], mx.at[e])
         c_xx(e).start()
-    flush(nz - 1)
+    flush(dord(nz - 1))
 
     c_ik(0).wait_recv()
     gi_out[...] = gi[rows_of(c), :] + decode(rk[0], nk[0])
@@ -271,7 +299,9 @@
         c_ir(e).wait_send()
         c_ik(e).wait_send()
         c_xx(e).wait_send()
-    c_cz(1).wait_send()
+    own_line(lambda copy: copy.wait_send())
+    for t in range(1, nz):
+        pass_line(t, lambda copy: copy.wait_send())
     for e in range(1, nz):
         c_cr(e).wait_send()
         c_gy(e).wait_send()
@@ -284,7 +314,7 @@
     nz, nx = nr // 2, nc // 2
     f32 = jnp.float32
     dma = pltpu.SemaphoreType.DMA
-    pairs = [(), (nx,), (nx,), (), (nz,), (nz,), (nz,), (nz,), (nx,), (nx,)]
+    pairs = [(), (nx,), (nx,), (), (nz + 1,), (nz,), (nz,), (nz,), (nx,), (nx,)]
     pairs += [(nz,), (nz,), (nx,), (nx,)]
     sems = []
     for shape in pairs:

time: 45.4 us -> 47.8 us (1.053)
  Pallas kernels: 40.5 us -> 42.9 us
    pallas_call x1, Pallas kernels: 40.5 us -> 42.9 us  [shards(): pl.pallas_call(functools.partial(kernel, nr, nc), out_shape=(jax.ShapeDty...]
where the time goes in v4:
time: 47.8 us; the launch traced here: 47.6 us
  Pallas kernels  42.9 us (90%)
  local copies, waits for them, and re-layouts  4.03 us (8%)
  between operations  0.65 us (1%)
    pallas_call x1, Pallas kernels, shards(): pl.pallas_call(functools.partial(kernel, nr, nc), out_shape=(jax.ShapeDty...  42.9 us
    unnamed x8, local copies, waits for them, and re-layouts  4.03 us

profile of v4, /device:TPU:0, one launch (start us, length us, event | category | flops | bytes accessed | tf_op | source)
XLA Modules:
  0.0 47.6 jit_solution(3251897104040961755)
XLA Ops:
  0.6 0.0 copy-start
  0.6 0.9 %copy-done = bf16[512,256]{1,0:T(8,128)(2,1)S(1)} copy-done((bf16[512,256]{1,0:T(8,128)(2,1)S(1)}, bf16[512,256]{1,0:T(8,128)(2,1)}, u32[]{:S(2)}) %copy-start) | copy-done | bytes 262168
  1.6 0.0 copy-start.1
  1.6 0.9 %copy-done.1 = bf16[256,256]{1,0:T(8,128)(2,1)S(1)} copy-done((bf16[256,256]{1,0:T(8,128)(2,1)S(1)}, bf16[256,256]{1,0:T(8,128)(2,1)}, u32[]{:S(2)}) %copy-start.1) | copy-done | bytes 131096
  2.5 0.0 copy-start.2
  2.5 0.7 %copy-done.2 = s32[1,1,4,4]{3,2,1,0:T(4,128)S(1)} copy-done((s32[1,1,4,4]{3,2,1,0:T(4,128)S(1)}, s32[1,1,4,4]{3,2,1,0:T(4,128)}, u32[]{:S(2)}) %copy-start.2) | copy-done | bytes 88
  3.2 42.9 %shard_map.50 = (f32[512,256]{1,0:T(8,128)S(1)}, f32[256,256]{1,0:T(8,128)S(1)}) custom-call(bf16[512,256]{1,0:T(8,128)(2,1)S(1)} %copy-done, bf16[256,256]{1,0:T(8,128)(2,1)S(1)} %copy-done.1, s32[1,1,4,4]{3,2,1,0:T(4,128)S(1)} %copy-done.2), custom_call_target="tpu_custom_call" | custom-call | tf_op jit(solution)/shard_map/pallas_call | solution.py:323
  46.1 0.8 %copy.7 = f32[512,256]{1,0:T(8,128)} copy(f32[512,256]{1,0:T(8,128)S(1)} %get-tuple-element.4) | data formatting | bytes 1048576
  46.9 0.7 %copy.8 = f32[256,256]{1,0:T(8,128)} copy(f32[256,256]{1,0:T(8,128)S(1)} %get-tuple-element.5) | data formatting | bytes 524288
Async XLA Ops:
  0.6 1.0 %copy-start = (bf16[512,256]{1,0:T(8,128)(2,1)S(1)}, bf16[512,256]{1,0:T(8,128)(2,1)}, u32[]{:S(2)}) copy-start(bf16[512,256]{1,0:T(8,128)(2,1)} %items_ref.1) | copy-start | bytes 786436
  1.6 0.9 %copy-start.1 = (bf16[256,256]{1,0:T(8,128)(2,1)S(1)}, bf16[256,256]{1,0:T(8,128)(2,1)}, u32[]{:S(2)}) copy-start(bf16[256,256]{1,0:T(8,128)(2,1)} %ctx_ref.1) | copy-start | bytes 393220
  2.5 0.7 %copy-start.2 = (s32[1,1,4,4]{3,2,1,0:T(4,128)S(1)}, s32[1,1,4,4]{3,2,1,0:T(4,128)}, u32[]{:S(2)}) copy-start(s32[1,1,4,4]{3,2,1,0:T(4,128)} %tiles_ref.1) | copy-start | bytes 196

commit v5 on v3

--- a/solution.py
+++ b/solution.py
@@ -213,6 +213,11 @@
 
         block(zof(d) * 2 + y, gco.at[d])
         c_cr(d).wait_recv()
+
+        @pl.when(d == nz - 1)
+        def _():
+            c_gy(0).start()
+
         block(zof(d) * 2 + 1 - y, gct)
         encode(gct[...], qy.at[d], my.at[d])
         c_gy(d).start()
@@ -224,7 +229,6 @@
         return carry
 
     lax.fori_loop(1, nz, zstep, 0)
-    c_gy(0).start()
 
     def rows_of(i):
         return pl.ds(pl.multiple_of(i * bi, bi), bi)

time: 45.4 us -> 46.7 us (1.029)
  Pallas kernels: 40.5 us -> 41.8 us
    pallas_call x1, Pallas kernels: 40.5 us -> 41.8 us  [shards(): pl.pallas_call(functools.partial(kernel, nr, nc), out_shape=(jax.ShapeDty...]
where the time goes in v5:
time: 46.7 us; the launch traced here: 46.5 us
  Pallas kernels  41.8 us (90%)
  local copies, waits for them, and re-layouts  4.03 us (9%)
  between operations  0.65 us (1%)
    pallas_call x1, Pallas kernels, shards(): pl.pallas_call(functools.partial(kernel, nr, nc), out_shape=(jax.ShapeDty...  41.8 us
    unnamed x8, local copies, waits for them, and re-layouts  4.03 us

profile of v5, /device:TPU:0, one launch (start us, length us, event | category | flops | bytes accessed | tf_op | source)
XLA Modules:
  0.0 46.5 jit_solution(9447840331558242365)
XLA Ops:
  0.6 0.0 copy-start
  0.6 0.9 %copy-done = bf16[512,256]{1,0:T(8,128)(2,1)S(1)} copy-done((bf16[512,256]{1,0:T(8,128)(2,1)S(1)}, bf16[512,256]{1,0:T(8,128)(2,1)}, u32[]{:S(2)}) %copy-start) | copy-done | bytes 262168
  1.6 0.0 copy-start.1
  1.6 0.9 %copy-done.1 = bf16[256,256]{1,0:T(8,128)(2,1)S(1)} copy-done((bf16[256,256]{1,0:T(8,128)(2,1)S(1)}, bf16[256,256]{1,0:T(8,128)(2,1)}, u32[]{:S(2)}) %copy-start.1) | copy-done | bytes 131096
  2.5 0.0 copy-start.2
  2.5 0.7 %copy-done.2 = s32[1,1,4,4]{3,2,1,0:T(4,128)S(1)} copy-done((s32[1,1,4,4]{3,2,1,0:T(4,128)S(1)}, s32[1,1,4,4]{3,2,1,0:T(4,128)}, u32[]{:S(2)}) %copy-start.2) | copy-done | bytes 88
  3.2 41.8 %shard_map.50 = (f32[512,256]{1,0:T(8,128)S(1)}, f32[256,256]{1,0:T(8,128)S(1)}) custom-call(bf16[512,256]{1,0:T(8,128)(2,1)S(1)} %copy-done, bf16[256,256]{1,0:T(8,128)(2,1)S(1)} %copy-done.1, s32[1,1,4,4]{3,2,1,0:T(4,128)S(1)} %copy-done.2), custom_call_target="tpu_custom_call" | custom-call | tf_op jit(solution)/shard_map/pallas_call | solution.py:297
  45.0 0.8 %copy.7 = f32[512,256]{1,0:T(8,128)} copy(f32[512,256]{1,0:T(8,128)S(1)} %get-tuple-element.4) | data formatting | bytes 1048576
  45.8 0.7 %copy.8 = f32[256,256]{1,0:T(8,128)} copy(f32[256,256]{1,0:T(8,128)S(1)} %get-tuple-element.5) | data formatting | bytes 524288
Async XLA Ops:
  0.6 1.0 %copy-start = (bf16[512,256]{1,0:T(8,128)(2,1)S(1)}, bf16[512,256]{1,0:T(8,128)(2,1)}, u32[]{:S(2)}) copy-start(bf16[512,256]{1,0:T(8,128)(2,1)} %items_ref.1) | copy-start | bytes 786436
  1.6 0.9 %copy-start.1 = (bf16[256,256]{1,0:T(8,128)(2,1)S(1)}, bf16[256,256]{1,0:T(8,128)(2,1)}, u32[]{:S(2)}) copy-start(bf16[256,256]{1,0:T(8,128)(2,1)} %ctx_ref.1) | copy-start | bytes 393220
  2.5 0.7 %copy-start.2 = (s32[1,1,4,4]{3,2,1,0:T(4,128)S(1)}, s32[1,1,4,4]{3,2,1,0:T(4,128)}, u32[]{:S(2)}) copy-start(s32[1,1,4,4]{3,2,1,0:T(4,128)} %tiles_ref.1) | copy-start | bytes 196
